TPU v7x, 128 devices: a whole 4x4x4 slice. The times are simulated.
128 devices in a mesh: seq: 8 (over x, y_hi), tensor: 16 (over z, y_lo, core).
Axes of the slice: x: 4, y: 4 (y_hi: 2, y_lo: 2; y = y_hi * 2 + y_lo), z: 4, core: 2. Of those that a mesh axis runs over, the one named last changes fastest.
Arguments:
- activations: bfloat16 [8192, 2048], P('seq', 'tensor'), may hold values from -6 to 6
- bases: int32 [8192], P('seq'), may hold values from 0 to 4
- complement: int32 [5], replicated, may hold values from 0 to 4, each once
- embedding: bfloat16 [5, 2048], replicated, may hold values from -6 to 6
- filter_taps: bfloat16 [255, 2048], P(None, 'tensor'), may hold values from -0.375 to 0.375
- projection: bfloat16 [2048, 2048], P('tensor'), may hold values from -0.125 to 0.125
Outputs:
- mixed: bfloat16 [8192, 2048], P('seq', 'tensor')
Inputs may be any that keep to these rules, and one draw needn't show every extreme that they name: `complement`: each of the 5 ids appears once.
All inputs are finite; a program needn't handle non-finite values.
Results may differ from a plain program's by a relative error of at most 0.0085.
Values may be sent and summed in bfloat16 or wider, within the bound.
A program may use at most 320 MiB of HBM per device.

v0:
```python
import functools

import jax
import jax.numpy as jnp
import numpy as np
from jax import lax
from jax.experimental import pallas as pl
from jax.experimental.pallas import tpu as pltpu
from jax.sharding import PartitionSpec as P

MESH = pl.DeviceIdType.MESH
F32, BF16 = jnp.float32, jnp.bfloat16
LANES = 128
BLOCK = 256
WINDOW = 2 * BLOCK


def split_table(table):
    high = table.astype(BF16)
    low = (table - high.astype(np.float64)).astype(BF16)
    return high, low


def dft_tables(taps_count):
    frequency = np.arange(BLOCK)[:, None]
    place = np.arange(WINDOW)[None, :]
    angle = 2 * np.pi / WINDOW * (frequency * place % WINDOW)
    sines = -np.sin(angle)
    sines[0] = 1.0 - 2.0 * (np.arange(WINDOW) % 2)
    analysis = np.concatenate([np.cos(angle), sines], axis=0)
    taps_forward = analysis[:, :BLOCK].copy()
    taps_forward[:, taps_count:] = 0
    taps_backward = np.zeros((WINDOW, BLOCK))
    taps_backward[:, :taps_count] = taps_forward[:, :taps_count][:, ::-1]
    taps_tables = np.concatenate([taps_forward, taps_backward], axis=0)[:, :taps_count]
    out_place = np.arange(BLOCK)[:, None] + (BLOCK - taps_count)
    out_angle = 2 * np.pi / WINDOW * (out_place * np.arange(BLOCK)[None, :] % WINDOW)
    cosines = 2 * np.cos(out_angle) / WINDOW
    cosines[:, 0] = 1.0 / WINDOW
    sines = -2 * np.sin(out_angle) / WINDOW
    sines[:, 0] = (1.0 - 2.0 * (out_place[:, 0] % 2)) / WINDOW
    synthesis = np.concatenate([cosines, sines], axis=1)
    return *split_table(analysis), *split_table(taps_tables), *split_table(synthesis)


def dot(a, b):
    return jnp.dot(a, b, preferred_element_type=F32)


def gelu(v):
    return v * (0.5 + 0.5 * lax.erf(v * np.float32(np.sqrt(0.5))))


def kernel(
    acts_ref, bases_ref, complement_ref, embedding_ref, taps_ref, weight_ref,
    flip_ref, fwd_hi, fwd_lo, tap_hi, tap_lo, inv_hi, inv_lo,
    out_ref,
    halo, bases_halo, mirror, mirror_halo, weight_far,
    table, coef, rows, wide, near, far,
    two_send, two_plus, two_minus, plus_send, minus_send, plus_recv, minus_recv, y_send, y_recv, y_keep,
    send_sem, recv_sem,
):
    seq, tensor = lax.axis_index("seq"), lax.axis_index("tensor")
    seq_count = lax.axis_size("seq")
    z, y, core = tensor // 4, (tensor // 2) % 2, tensor % 2
    right, left = lax.rem(seq + 1, seq_count), lax.rem(seq + seq_count - 1, seq_count)
    opposite = 15 - tensor
    z_plus, z_minus, z_two = lax.rem(z + 1, 4), lax.rem(z + 3, 4), lax.rem(z + 2, 4)
    at_plus = (seq, z_plus * 4 + y * 2 + core)
    at_minus = (seq, z_minus * 4 + y * 2 + core)
    at_core = (seq, z * 4 + y * 2 + (1 - core))
    at_y = (seq, z * 4 + (1 - y) * 2 + core)
    partners = [
        (right, tensor), (left, tensor), (seq, opposite), (right, opposite), (left, opposite),
        at_plus, at_minus, at_core, at_y,
    ]
    barrier = pltpu.get_barrier_semaphore()
    for partner in partners:
        pl.semaphore_signal(barrier, inc=1, device_id=partner, device_id_type=MESH)
    pl.semaphore_wait(barrier, len(partners))

    count = [0]

    def send(source, target, device):
        index = count[0]
        count[0] += 1
        copy = pltpu.make_async_remote_copy(
            src_ref=source, dst_ref=target, send_sem=send_sem.at[index], recv_sem=recv_sem.at[index],
            device_id=device, device_id_type=MESH,
        )
        copy.start()
        return copy

    length = acts_ref.shape[0]
    blocks = length // BLOCK
    first, last = pl.ds(0, LANES), pl.ds(length - LANES, LANES)
    starts = [send(acts_ref.at[last], mirror_halo.at[0], (right, opposite))]
    bounds = [0, 384, 640, 896, 1024]
    pieces = [
        send(acts_ref.at[pl.ds(a, b - a)], mirror.at[pl.ds(a, b - a)], (seq, opposite))
        for a, b in zip(bounds[:-1], bounds[1:])
    ]
    starts.append(send(acts_ref.at[first], mirror_halo.at[1], (left, opposite)))
    edges = [
        send(acts_ref.at[last], halo.at[0], (right, tensor)),
        send(bases_ref, bases_halo.at[0], (right, tensor)),
        send(acts_ref.at[first], halo.at[1], (left, tensor)),
        send(bases_ref, bases_halo.at[1], (left, tensor)),
    ]
    weight_copy = send(weight_ref, weight_far, at_core)

    taps = taps_ref[...]
    spectrum = dot(tap_hi[...], taps) + dot(tap_lo[...], taps)
    for strand in range(2):
        lanes = pl.ds(strand * LANES, LANES)
        real = spectrum[strand * WINDOW : strand * WINDOW + BLOCK]
        imag = spectrum[strand * WINDOW + BLOCK : (strand + 1) * WINDOW]
        top = lax.broadcasted_iota(jnp.int32, (BLOCK, LANES), 0) == 0
        coef[0, :, lanes] = real
        coef[1, :, lanes] = jnp.where(top, 0.0, imag)
        coef[2, :, lanes] = jnp.where(top, imag, real)

    own = embedding_ref[:, pl.ds(pl.multiple_of(tensor * LANES, LANES), LANES)].astype(F32)
    vocab = own.shape[0]
    table[...] = jnp.zeros_like(table)
    for base in range(vocab):
        table[base : base + 1, 0:LANES] = own[base : base + 1]
        row = jnp.zeros((1, LANES), F32)
        for other in range(vocab):
            weight = (complement_ref[base] == other).astype(F32)
            row = row + weight * own[other : other + 1]
        table[base : base + 1, LANES:] = row
    flip = flip_ref[...]

    def widen(source, half):
        for z_at in range(4):
            for y_at in range(2):
                chunk = z_at * 4 + y_at * 2 + core
                columns = pl.ds(pl.multiple_of(chunk * LANES, LANES), LANES)
                mirrored = pl.ds(pl.multiple_of((15 - chunk) * LANES, LANES), LANES)
                place = pl.ds(y_at * LANES, LANES)
                wide[z_at, pl.ds(half * BLOCK, LANES), place] = source[:, columns]
                wide[z_at, pl.ds(half * BLOCK + LANES, LANES), place] = dot(source[:, mirrored], flip).astype(BF16)

    widen(weight_ref, 0)
    bases_table = table[...].astype(BF16)

    def form_rows(group):
        if group == 0:
            plain, mirrored, ids = halo[0], mirror_halo[0], bases_halo[0, 7:8, :]
            keep = seq > 0
        elif group == 9:
            plain, mirrored, ids = halo[1], mirror_halo[1], bases_halo[1, 0:1, :]
            keep = seq < seq_count - 1
        else:
            part = pl.ds((group - 1) * LANES, LANES)
            plain, mirrored, ids = acts_ref[part], mirror[part], bases_ref[group - 1 : group, :]
            keep = None
        hot = (lax.broadcasted_iota(jnp.int32, (16, LANES), 0) == ids).astype(F32).astype(BF16)
        added = lax.dot_general(hot, bases_table, (((0,), (0,)), ((), ())), preferred_element_type=F32)
        both = jnp.concatenate([plain.astype(F32), dot(mirrored, flip)], axis=1) + added
        if keep is not None:
            both = jnp.where(keep, both, 0.0)
        rows[pl.ds(group * LANES, LANES), :] = both.astype(BF16)

    def conv(block):
        window = rows[pl.ds(block * BLOCK, WINDOW), :]
        field = dot(fwd_hi[...], window) + dot(fwd_lo[...], window)
        real, imag = field[:BLOCK], field[BLOCK:]
        cross = coef[1]
        product = jnp.concatenate([real * coef[0] + imag * cross, imag * coef[2] - real * cross], axis=0)
        high = product.astype(BF16)
        low = (product - high.astype(F32)).astype(BF16)
        filtered = dot(inv_hi[...], high) + dot(inv_lo[...], high) + dot(inv_hi[...], low)
        near[block] = gelu(filtered).astype(BF16)
        return send(near.at[block], far.at[block], at_core)

    def project(block, z_at, low, high):
        return dot(near[block, low:high, :], wide[z_at, 0:BLOCK, :]) + dot(
            far[block, low:high, :], wide[z_at, BLOCK:, :]
        )

    half = BLOCK // 2
    two, plain, added = {}, {}, {}

    def begin(block):
        two_send[block] = project(block, z_two, 0, BLOCK).astype(BF16)
        two[block] = (
            send(two_send.at[block, pl.ds(0, half)], two_plus.at[block], at_plus),
            send(two_send.at[block, pl.ds(half, half)], two_minus.at[block], at_minus),
        )
        plus_send[block, half:, :] = project(block, z_plus, half, BLOCK).astype(BF16)
        plain_plus = send(plus_send.at[block, pl.ds(half, half)], plus_recv.at[block, pl.ds(half, half)], at_plus)
        minus_send[block, :half, :] = project(block, z_minus, 0, half).astype(BF16)
        plain_minus = send(minus_send.at[block, pl.ds(0, half)], minus_recv.at[block, pl.ds(0, half)], at_minus)
        plain[block] = (plain_plus, plain_minus)

    def accumulate(block):
        two[block][0].wait_recv()
        total = project(block, z_plus, 0, half) + two_plus[block].astype(F32)
        plus_send[block, :half, :] = total.astype(BF16)
        added_plus = send(plus_send.at[block, pl.ds(0, half)], plus_recv.at[block, pl.ds(0, half)], at_plus)
        two[block][1].wait_recv()
        total = project(block, z_minus, half, BLOCK) + two_minus[block].astype(F32)
        minus_send[block, half:, :] = total.astype(BF16)
        added_minus = send(minus_send.at[block, pl.ds(half, half)], minus_recv.at[block, pl.ds(half, half)], at_minus)
        added[block] = (added_plus, added_minus)

    crossed = {}

    def finish(block):
        total = project(block, z, 0, BLOCK)
        for copy in plain[block] + added[block]:
            copy.wait_recv()
        total = total + plus_recv[block].astype(F32) + minus_recv[block].astype(F32)
        low, high = total[:, :LANES], total[:, LANES:]
        y_keep[block] = jnp.where(y == 0, low, high)
        y_send[block] = jnp.where(y == 0, high, low).astype(BF16)
        crossed[block] = send(y_send.at[block], y_recv.at[block], at_y)

    def emit(block):
        crossed[block].wait_recv()
        out_ref[pl.ds(block * BLOCK, BLOCK), :] = (y_keep[block] + y_recv[block].astype(F32)).astype(BF16)

    for copy in edges[:2]:
        copy.wait_recv()
    starts[0].wait_recv()
    pieces[0].wait_recv()
    for group in range(4):
        form_rows(group)
    cores = [conv(0)]
    pieces[1].wait_recv()
    form_rows(4)
    form_rows(5)
    cores.append(conv(1))
    weight_copy.wait_recv()
    widen(weight_far, 1)
    cores[0].wait_recv()
    begin(0)
    pieces[2].wait_recv()
    form_rows(6)
    form_rows(7)
    cores.append(conv(2))
    cores[1].wait_recv()
    begin(1)
    accumulate(0)
    for copy in edges[2:]:
        copy.wait_recv()
    pieces[3].wait_recv()
    starts[1].wait_recv()
    form_rows(8)
    form_rows(9)
    cores.append(conv(3))
    cores[2].wait_recv()
    begin(2)
    accumulate(1)
    finish(0)
    cores[3].wait_recv()
    begin(3)
    accumulate(2)
    finish(1)
    emit(0)
    accumulate(3)
    finish(2)
    emit(1)
    finish(3)
    emit(2)
    emit(3)
    for copy in starts + pieces + edges + [weight_copy] + cores:
        copy.wait_send()
    for block in range(blocks):
        for copy in two[block] + plain[block] + added[block] + (crossed[block],):
            copy.wait_send()


def body(activations, bases, complement, embedding, filter_taps, projection):
    length, channels = activations.shape
    blocks = length // BLOCK
    copies = 11 + 8 * blocks
    tables = dft_tables(filter_taps.shape[0])
    flip = np.eye(LANES)[::-1].astype(BF16)
    vmem = pl.BlockSpec(memory_space=pltpu.VMEM)
    return pl.pallas_call(
        kernel,
        out_shape=jax.ShapeDtypeStruct((length, channels), BF16),
        in_specs=[vmem, vmem, pl.BlockSpec(memory_space=pltpu.SMEM)] + [vmem] * 10,
        out_specs=vmem,
        scratch_shapes=[
            pltpu.VMEM((2, LANES, LANES), BF16),
            pltpu.VMEM((2, 8, LANES), jnp.int32),
            pltpu.VMEM((length, LANES), BF16),
            pltpu.VMEM((2, LANES, LANES), BF16),
            pltpu.VMEM(projection.shape, BF16),
            pltpu.VMEM((16, 2 * LANES), F32),
            pltpu.VMEM((3, BLOCK, 2 * LANES), F32),
            pltpu.VMEM((length + 2 * LANES, 2 * LANES), BF16),
            pltpu.VMEM((4, 4 * LANES, 2 * LANES), BF16),
            pltpu.VMEM((blocks, BLOCK, 2 * LANES), BF16),
            pltpu.VMEM((blocks, BLOCK, 2 * LANES), BF16),
            pltpu.VMEM((blocks, BLOCK, 2 * LANES), BF16),
            pltpu.VMEM((blocks, BLOCK // 2, 2 * LANES), BF16),
            pltpu.VMEM((blocks, BLOCK // 2, 2 * LANES), BF16),
            pltpu.VMEM((blocks, BLOCK, 2 * LANES), BF16),
            pltpu.VMEM((blocks, BLOCK, 2 * LANES), BF16),
            pltpu.VMEM((blocks, BLOCK, 2 * LANES), BF16),
            pltpu.VMEM((blocks, BLOCK, 2 * LANES), BF16),
            pltpu.VMEM((blocks, BLOCK, LANES), BF16),
            pltpu.VMEM((blocks, BLOCK, LANES), BF16),
            pltpu.VMEM((blocks, BLOCK, LANES), F32),
            pltpu.SemaphoreType.DMA((copies,)),
            pltpu.SemaphoreType.DMA((copies,)),
        ],
        compiler_params=pltpu.CompilerParams(
            collective_id=0, has_side_effects=True, vmem_limit_bytes=48 * 1024 * 1024
        ),
    )(
        activations, bases.reshape(length // LANES, LANES), complement, embedding, filter_taps, projection,
        jnp.asarray(flip), *[jnp.asarray(t) for t in tables],
    )


def solution(mesh):
    placed = (P("seq", "tensor"), P("seq"), P(), P(), P(None, "tensor"), P("tensor", None))
    return jax.shard_map(
        body, mesh=mesh, in_specs=placed, out_specs=P("seq", "tensor"), check_vma=False
    )
```

profile of v0, /device:TPU:16, one launch (start us, length us, event | category | flops | bytes accessed | tf_op | source)
XLA Modules:
  0.0 56.5 jit_solution(10363308624206626847)
XLA Ops:
  0.0 0.0 copy-start.12
  0.0 0.7 %copy-done.12 = s32[5]{0:T(128)S(1)} copy-done((s32[5]{0:T(128)S(1)}, s32[5]{0:T(128)}, u32[]{:S(2)}) %copy-start.12) | copy-done | bytes 44
  0.7 0.0 copy-start
  0.7 1.0 %copy-done = bf16[128,2048]{1,0:T(8,128)(2,1)S(1)} copy-done((bf16[128,2048]{1,0:T(8,128)(2,1)S(1)}, bf16[128,2048]{1,0:T(8,128)(2,1)}, u32[]{:S(2)}) %copy-start) | copy-done | bytes 524312
  1.7 0.0 copy-start.1
  1.7 1.0 %copy-done.1 = bf16[1024,255]{1,0:T(8,128)(2,1)S(1)} copy-done((bf16[1024,255]{1,0:T(8,128)(2,1)S(1)}, bf16[1024,255]{1,0:T(8,128)(2,1)}, u32[]{:S(2)}) %copy-start.1) | copy-done | bytes 522264
  2.7 0.0 copy-start.2
  2.7 1.0 %copy-done.2 = bf16[1024,255]{1,0:T(8,128)(2,1)S(1)} copy-done((bf16[1024,255]{1,0:T(8,128)(2,1)S(1)}, bf16[1024,255]{1,0:T(8,128)(2,1)}, u32[]{:S(2)}) %copy-start.2) | copy-done | bytes 522264
  3.8 0.0 copy-start.3
  3.8 1.0 %copy-done.3 = bf16[512,512]{1,0:T(8,128)(2,1)S(1)} copy-done((bf16[512,512]{1,0:T(8,128)(2,1)S(1)}, bf16[512,512]{1,0:T(8,128)(2,1)}, u32[]{:S(2)}) %copy-start.3) | copy-done | bytes 524312
  4.8 0.0 copy-start.4
  4.8 1.0 %copy-done.4 = bf16[512,512]{1,0:T(8,128)(2,1)S(1)} copy-done((bf16[512,512]{1,0:T(8,128)(2,1)S(1)}, bf16[512,512]{1,0:T(8,128)(2,1)}, u32[]{:S(2)}) %copy-start.4) | copy-done | bytes 524312
  5.9 0.0 copy-start.5
  5.9 0.9 %copy-done.5 = bf16[1024,128]{1,0:T(8,128)(2,1)S(1)} copy-done((bf16[1024,128]{1,0:T(8,128)(2,1)S(1)}, bf16[1024,128]{1,0:T(8,128)(2,1)}, u32[]{:S(2)}) %copy-start.5) | copy-done | bytes 262168
  6.8 0.0 copy-start.6
  6.8 0.9 %copy-done.6 = bf16[256,512]{1,0:T(8,128)(2,1)S(1)} copy-done((bf16[256,512]{1,0:T(8,128)(2,1)S(1)}, bf16[256,512]{1,0:T(8,128)(2,1)}, u32[]{:S(2)}) %copy-start.6) | copy-done | bytes 262168
  7.8 0.0 copy-start.7
  7.8 0.9 %copy-done.7 = bf16[256,512]{1,0:T(8,128)(2,1)S(1)} copy-done((bf16[256,512]{1,0:T(8,128)(2,1)S(1)}, bf16[256,512]{1,0:T(8,128)(2,1)}, u32[]{:S(2)}) %copy-start.7) | copy-done | bytes 262168
  8.7 0.0 copy-start.8
  8.7 0.8 %copy-done.8 = bf16[255,128]{1,0:T(8,128)(2,1)S(1)} copy-done((bf16[255,128]{1,0:T(8,128)(2,1)S(1)}, bf16[255,128]{1,0:T(8,128)(2,1)}, u32[]{:S(2)}) %copy-start.8) | copy-done | bytes 65304
  9.6 0.0 copy-start.9
  9.6 0.8 %copy-done.9 = bf16[5,2048]{1,0:T(8,128)(2,1)S(1)} copy-done((bf16[5,2048]{1,0:T(8,128)(2,1)S(1)}, bf16[5,2048]{1,0:T(8,128)(2,1)}, u32[]{:S(2)}) %copy-start.9) | copy-done | bytes 20504
  10.3 0.0 copy-start.10
  10.3 0.8 %copy-done.10 = bf16[128,128]{1,0:T(8,128)(2,1)S(1)} copy-done((bf16[128,128]{1,0:T(8,128)(2,1)S(1)}, bf16[128,128]{1,0:T(8,128)(2,1)}, u32[]{:S(2)}) %copy-start.10) | copy-done | bytes 32792
  11.1 0.0 copy-start.11
  11.1 0.7 %copy-done.11 = s32[1024]{0:T(1024)S(1)} copy-done((s32[1024]{0:T(1024)S(1)}, s32[1024]{0:T(1024)}, u32[]{:S(2)}) %copy-start.11) | copy-done | bytes 4120
  11.8 44.0 %shard_map.127 = bf16[1024,128]{1,0:T(8,128)(2,1)S(1)} custom-call(bf16[1024,128]{1,0:T(8,128)(2,1)S(1)} %copy-done.5, s32[8,128]{1,0:T(8,128)S(1)} %bitcast.1, s32[5]{0:T(128)S(1)} %copy-done.12, bf16[5,2048]{1,0:T(8,128)(2,1)S(1)} %copy-done.9, bf16[255,128]{1,0:T(8,128)(2,1)S(1)} %copy-done.8, bf16[128,2048]{1,0:T(8,128)(2,1)S(1)} %copy-done, ...), custom_call_target="tpu_custom_call" | custom-call | tf_op jit(solution)/shard_map/pallas_call | solution.py:283
  55.8 0.7 %copy.15 = bf16[1024,128]{1,0:T(8,128)(2,1)} copy(bf16[1024,128]{1,0:T(8,128)(2,1)S(1)} %shard_map.127) | data formatting | bytes 524288
Async XLA Ops:
  0.0 0.7 %copy-start.12 = (s32[5]{0:T(128)S(1)}, s32[5]{0:T(128)}, u32[]{:S(2)}) copy-start(s32[5]{0:T(128)} %complement_ref.1) | copy-start | bytes 64
  0.7 1.0 %copy-start = (bf16[128,2048]{1,0:T(8,128)(2,1)S(1)}, bf16[128,2048]{1,0:T(8,128)(2,1)}, u32[]{:S(2)}) copy-start(bf16[128,2048]{1,0:T(8,128)(2,1)} %weight_ref.1) | copy-start | bytes 1572868
  1.7 1.0 %copy-start.1 = (bf16[1024,255]{1,0:T(8,128)(2,1)S(1)}, bf16[1024,255]{1,0:T(8,128)(2,1)}, u32[]{:S(2)}) copy-start(bf16[1024,255]{1,0:T(8,128)(2,1)} %constant.18.clone.tap_lo) | copy-start | bytes 1566724
  2.7 1.0 %copy-start.2 = (bf16[1024,255]{1,0:T(8,128)(2,1)S(1)}, bf16[1024,255]{1,0:T(8,128)(2,1)}, u32[]{:S(2)}) copy-start(bf16[1024,255]{1,0:T(8,128)(2,1)} %constant.17.clone.tap_hi) | copy-start | bytes 1566724
  3.8 1.0 %copy-start.3 = (bf16[512,512]{1,0:T(8,128)(2,1)S(1)}, bf16[512,512]{1,0:T(8,128)(2,1)}, u32[]{:S(2)}) copy-start(bf16[512,512]{1,0:T(8,128)(2,1)} %constant.16.clone.fwd_lo) | copy-start | bytes 1572868
  4.8 1.0 %copy-start.4 = (bf16[512,512]{1,0:T(8,128)(2,1)S(1)}, bf16[512,512]{1,0:T(8,128)(2,1)}, u32[]{:S(2)}) copy-start(bf16[512,512]{1,0:T(8,128)(2,1)} %constant.15.clone.fwd_hi) | copy-start | bytes 1572868
  5.9 0.9 %copy-start.5 = (bf16[1024,128]{1,0:T(8,128)(2,1)S(1)}, bf16[1024,128]{1,0:T(8,128)(2,1)}, u32[]{:S(2)}) copy-start(bf16[1024,128]{1,0:T(8,128)(2,1)} %acts_ref.1) | copy-start | bytes 786436
  6.8 0.9 %copy-start.6 = (bf16[256,512]{1,0:T(8,128)(2,1)S(1)}, bf16[256,512]{1,0:T(8,128)(2,1)}, u32[]{:S(2)}) copy-start(bf16[256,512]{1,0:T(8,128)(2,1)} %constant.20.clone.inv_lo) | copy-start | bytes 786436
  7.8 0.9 %copy-start.7 = (bf16[256,512]{1,0:T(8,128)(2,1)S(1)}, bf16[256,512]{1,0:T(8,128)(2,1)}, u32[]{:S(2)}) copy-start(bf16[256,512]{1,0:T(8,128)(2,1)} %constant.19.clone.inv_hi) | copy-start | bytes 786436
  8.7 0.8 %copy-start.8 = (bf16[255,128]{1,0:T(8,128)(2,1)S(1)}, bf16[255,128]{1,0:T(8,128)(2,1)}, u32[]{:S(2)}) copy-start(bf16[255,128]{1,0:T(8,128)(2,1)} %taps_ref.1) | copy-start | bytes 195844
  9.6 0.8 %copy-start.9 = (bf16[5,2048]{1,0:T(8,128)(2,1)S(1)}, bf16[5,2048]{1,0:T(8,128)(2,1)}, u32[]{:S(2)}) copy-start(bf16[5,2048]{1,0:T(8,128)(2,1)} %embedding_ref.1) | copy-start | bytes 61444
  10.3 0.8 %copy-start.10 = (bf16[128,128]{1,0:T(8,128)(2,1)S(1)}, bf16[128,128]{1,0:T(8,128)(2,1)}, u32[]{:S(2)}) copy-start(bf16[128,128]{1,0:T(8,128)(2,1)} %constant.14.clone.flip_ref) | copy-start | bytes 98308
  11.1 0.7 %copy-start.11 = (s32[1024]{0:T(1024)S(1)}, s32[1024]{0:T(1024)}, u32[]{:S(2)}) copy-start(s32[1024]{0:T(1024)} %param.14) | copy-start | bytes 12292
where the time goes:
time: 57.1 us; the launch traced here: 56.5 us
  Pallas kernels  44 us (77%)
  local copies, waits for them, and re-layouts  12.5 us (22%)
    pallas_call x1, Pallas kernels, body(): pl.pallas_call(kernel, out_shape=jax.ShapeDtypeStruct((length, channels),...  44 us
    unnamed x27, local copies, waits for them, and re-layouts  12.5 us

commit v1 on v0

v1 whole, which is shorter than its diff:
```python
import functools

import jax
import jax.numpy as jnp
import numpy as np
from jax import lax
from jax.experimental import pallas as pl
from jax.experimental.pallas import tpu as pltpu
from jax.sharding import PartitionSpec as P

MESH = pl.DeviceIdType.MESH
F32, BF16 = jnp.float32, jnp.bfloat16
LANES = 128
BLOCK = 256
WINDOW = 2 * BLOCK


def split_table(table):
    high = table.astype(BF16)
    low = (table - high.astype(np.float64)).astype(BF16)
    return high, low


def dft_tables(taps_count):
    frequency = np.arange(BLOCK)[:, None]
    place = np.arange(WINDOW)[None, :]
    angle = 2 * np.pi / WINDOW * (frequency * place % WINDOW)
    sines = -np.sin(angle)
    sines[0] = 1.0 - 2.0 * (np.arange(WINDOW) % 2)
    analysis = np.concatenate([np.cos(angle), sines], axis=0)
    taps_forward = analysis[:, :BLOCK].copy()
    taps_forward[:, taps_count:] = 0
    taps_backward = np.zeros((WINDOW, BLOCK))
    taps_backward[:, :taps_count] = taps_forward[:, :taps_count][:, ::-1]
    taps_tables = np.concatenate([taps_forward, taps_backward], axis=0)[:, :taps_count]
    out_place = np.arange(BLOCK)[:, None] + (BLOCK - taps_count)
    out_angle = 2 * np.pi / WINDOW * (out_place * np.arange(BLOCK)[None, :] % WINDOW)
    cosines = 2 * np.cos(out_angle) / WINDOW
    cosines[:, 0] = 1.0 / WINDOW
    sines = -2 * np.sin(out_angle) / WINDOW
    sines[:, 0] = (1.0 - 2.0 * (out_place[:, 0] % 2)) / WINDOW
    synthesis = np.concatenate([cosines, sines], axis=1)
    return *split_table(analysis), *split_table(taps_tables), *split_table(synthesis)


def dot(a, b):
    return jnp.dot(a, b, preferred_element_type=F32)


def gelu(v):
    return v * (0.5 + 0.5 * lax.erf(v * np.float32(np.sqrt(0.5))))


def kernel(
    acts_hbm, bases_hbm, complement_hbm, embedding_hbm, taps_hbm, weight_hbm,
    flip_hbm, fwd_hi_hbm, fwd_lo_hbm, tap_hi_hbm, tap_lo_hbm, inv_hi_hbm, inv_lo_hbm,
    out_ref,
    acts_ref, bases_ref, complement_ref, embedding_ref, taps_ref, weight_ref,
    flip_ref, fwd_hi, fwd_lo, tap_hi, tap_lo, inv_hi, inv_lo,
    halo, bases_halo, mirror, mirror_halo, weight_far,
    table, coef, rows, wide, cross, near, far,
    two_send, two_plus, two_minus, plus_send, minus_send, plus_recv, minus_recv, y_send, y_recv, y_keep,
    early_send, early_recv, early_sum, late_two, late_two_plus, late_two_minus,
    late_plus_send, late_minus_send, late_plus, late_minus,
    send_sem, recv_sem, local_sem,
):
    fetched = []
    for source, target in (
        (taps_hbm, taps_ref), (tap_hi_hbm, tap_hi), (tap_lo_hbm, tap_lo), (complement_hbm, complement_ref),
        (embedding_hbm, embedding_ref), (flip_hbm, flip_ref), (weight_hbm, weight_ref), (bases_hbm, bases_ref),
        (acts_hbm, acts_ref), (fwd_hi_hbm, fwd_hi), (fwd_lo_hbm, fwd_lo), (inv_hi_hbm, inv_hi), (inv_lo_hbm, inv_lo),
    ):
        copy = pltpu.make_async_copy(source, target, local_sem.at[len(fetched)])
        copy.start()
        fetched.append(copy)

    def fetch(count):
        for copy in fetched[:count]:
            copy.wait()
        del fetched[:count]

    seq, tensor = lax.axis_index("seq"), lax.axis_index("tensor")
    seq_count = lax.axis_size("seq")
    z, y, core = tensor // 4, (tensor // 2) % 2, tensor % 2
    has_right, has_left = seq < seq_count - 1, seq > 0
    right, left = jnp.minimum(seq + 1, seq_count - 1), jnp.maximum(seq - 1, 0)
    opposite = 15 - tensor
    z_plus, z_minus, z_two = lax.rem(z + 1, 4), lax.rem(z + 3, 4), lax.rem(z + 2, 4)
    at_plus = (seq, z_plus * 4 + y * 2 + core)
    at_minus = (seq, z_minus * 4 + y * 2 + core)
    at_core = (seq, z * 4 + y * 2 + (1 - core))
    at_y = (seq, z * 4 + (1 - y) * 2 + core)
    barrier = pltpu.get_barrier_semaphore()

    def greet(*partners):
        for partner in partners:
            pl.semaphore_signal(barrier, inc=1, device_id=partner, device_id_type=MESH)

    greet((seq, opposite), at_plus, at_minus, at_core, at_y)
    pl.when(has_right)(lambda: greet((right, tensor), (right, opposite)))
    pl.when(has_left)(lambda: greet((left, tensor), (left, opposite)))
    pl.semaphore_wait(barrier, 5 + 2 * has_right.astype(jnp.int32) + 2 * has_left.astype(jnp.int32))

    count = [0]

    def plan(source, target, device):
        index = count[0]
        count[0] += 1
        return pltpu.make_async_remote_copy(
            src_ref=source, dst_ref=target, send_sem=send_sem.at[index], recv_sem=recv_sem.at[index],
            device_id=device, device_id_type=MESH,
        )

    def send(source, target, device):
        copy = plan(source, target, device)
        copy.start()
        return copy

    length = acts_hbm.shape[0]
    first, last = pl.ds(0, LANES), pl.ds(length - LANES, LANES)
    to_right = [
        plan(acts_hbm.at[last], mirror_halo.at[0], (right, opposite)),
        plan(acts_hbm.at[last], halo.at[0], (right, tensor)),
        plan(bases_hbm, bases_halo.at[0], (right, tensor)),
    ]
    to_left = [
        plan(acts_hbm.at[first], mirror_halo.at[1], (left, opposite)),
        plan(acts_hbm.at[first], halo.at[1], (left, tensor)),
        plan(bases_hbm, bases_halo.at[1], (left, tensor)),
    ]

    def each(copies, what):
        for copy in copies:
            getattr(copy, what)()

    bounds = [0, 384, 640, 896, 1024]
    pl.when(has_right)(lambda: each(to_right, "start"))
    pieces = [
        send(acts_hbm.at[pl.ds(a, b - a)], mirror.at[pl.ds(a, b - a)], (seq, opposite))
        for a, b in zip(bounds[:-1], bounds[1:])
    ]
    pl.when(has_left)(lambda: each(to_left, "start"))
    weight_copy = send(weight_hbm, weight_far, at_core)

    def blank(side):
        halo[side] = jnp.zeros_like(halo[side])
        mirror_halo[side] = jnp.zeros_like(mirror_halo[side])
        bases_halo[side] = jnp.zeros_like(bases_halo[side])

    pl.when(jnp.logical_not(has_left))(lambda: blank(0))
    pl.when(jnp.logical_not(has_right))(lambda: blank(1))

    fetch(3)
    taps = taps_ref[...]
    spectrum = dot(tap_hi[...], taps) + dot(tap_lo[...], taps)
    for strand in range(2):
        lanes = pl.ds(strand * LANES, LANES)
        real = spectrum[strand * WINDOW : strand * WINDOW + BLOCK]
        imag = spectrum[strand * WINDOW + BLOCK : (strand + 1) * WINDOW]
        top = lax.broadcasted_iota(jnp.int32, (BLOCK, LANES), 0) == 0
        coef[0, :, lanes] = real
        coef[1, :, lanes] = jnp.where(top, 0.0, imag)
        coef[2, :, lanes] = jnp.where(top, imag, real)

    fetch(3)
    own = embedding_ref[:, pl.ds(pl.multiple_of(tensor * LANES, LANES), LANES)].astype(F32)
    vocab = own.shape[0]
    table[...] = jnp.zeros_like(table)
    for base in range(vocab):
        table[base : base + 1, 0:LANES] = own[base : base + 1]
        row = jnp.zeros((1, LANES), F32)
        for other in range(vocab):
            weight = (complement_ref[base] == other).astype(F32)
            row = row + weight * own[other : other + 1]
        table[base : base + 1, LANES:] = row
    bases_table = table[...].astype(BF16)
    flip = flip_ref[...]

    def widen(source, half):
        for z_at in range(4):
            for y_at in range(2):
                chunk = z_at * 4 + y_at * 2 + core
                columns = pl.ds(pl.multiple_of(chunk * LANES, LANES), LANES)
                mirrored = pl.ds(pl.multiple_of((15 - chunk) * LANES, LANES), LANES)
                straight, turned = source[:, columns], dot(source[:, mirrored], flip).astype(BF16)
                for part, offset in ((straight, 0), (turned, LANES)):
                    depth = pl.ds(half * BLOCK + offset, LANES)
                    wide[z_at, depth, pl.ds(y_at * LANES, LANES)] = part
                    cross[y_at, depth, pl.ds(z_at * LANES, LANES)] = part

    fetch(1)
    widen(weight_ref, 0)

    def form_rows(group):
        if group == 0:
            plain, mirrored, ids = halo[0], mirror_halo[0], bases_halo[0, 7:8, :]
            keep = has_left
        elif group == 9:
            plain, mirrored, ids = halo[1], mirror_halo[1], bases_halo[1, 0:1, :]
            keep = has_right
        else:
            part = pl.ds((group - 1) * LANES, LANES)
            plain, mirrored, ids = acts_ref[part], mirror[part], bases_ref[group - 1 : group, :]
            keep = None
        hot = (lax.broadcasted_iota(jnp.int32, (16, LANES), 0) == ids).astype(F32).astype(BF16)
        added = lax.dot_general(hot, bases_table, (((0,), (0,)), ((), ())), preferred_element_type=F32)
        both = jnp.concatenate([plain.astype(F32), dot(mirrored, flip)], axis=1) + added
        if keep is not None:
            both = jnp.where(keep, both, 0.0)
        rows[pl.ds(group * LANES, LANES), :] = both.astype(BF16)

    def conv(block):
        window = rows[pl.ds(block * BLOCK, WINDOW), :]
        field = dot(fwd_hi[...], window) + dot(fwd_lo[...], window)
        real, imag = field[:BLOCK], field[BLOCK:]
        shared = coef[1]
        product = jnp.concatenate([real * coef[0] + imag * shared, imag * coef[2] - real * shared], axis=0)
        high = product.astype(BF16)
        low = (product - high.astype(F32)).astype(BF16)
        filtered = dot(inv_hi[...], high) + dot(inv_lo[...], high) + dot(inv_hi[...], low)
        near[block] = gelu(filtered).astype(BF16)
        return send(near.at[block], far.at[block], at_core)

    def project(block, weights, low, high):
        return dot(near[block, low:high, :], weights[0:BLOCK, :]) + dot(far[block, low:high, :], weights[BLOCK:, :])

    half = BLOCK // 2
    top, bottom = pl.ds(0, half), pl.ds(half, half)
    two, plain, added, crossed = {}, {}, {}, {}

    def begin(block):
        two_send[block] = project(block, wide.at[z_two], 0, BLOCK).astype(BF16)
        two[block] = (
            send(two_send.at[block, top], two_plus.at[block], at_plus),
            send(two_send.at[block, bottom], two_minus.at[block], at_minus),
        )
        plus_send[block, half:, :] = project(block, wide.at[z_plus], half, BLOCK).astype(BF16)
        plain_plus = send(plus_send.at[block, bottom], plus_recv.at[block, bottom], at_plus)
        minus_send[block, :half, :] = project(block, wide.at[z_minus], 0, half).astype(BF16)
        plain_minus = send(minus_send.at[block, top], minus_recv.at[block, top], at_minus)
        plain[block] = (plain_plus, plain_minus)

    def accumulate(block):
        total = project(block, wide.at[z_plus], 0, half)
        two[block][0].wait_recv()
        plus_send[block, :half, :] = (total + two_plus[block].astype(F32)).astype(BF16)
        added_plus = send(plus_send.at[block, top], plus_recv.at[block, top], at_plus)
        total = project(block, wide.at[z_minus], half, BLOCK)
        two[block][1].wait_recv()
        minus_send[block, half:, :] = (total + two_minus[block].astype(F32)).astype(BF16)
        added_minus = send(minus_send.at[block, bottom], minus_recv.at[block, bottom], at_minus)
        added[block] = (added_plus, added_minus)

    def finish(block):
        total = project(block, wide.at[z], 0, BLOCK)
        for copy in plain[block] + added[block]:
            copy.wait_recv()
        total = total + plus_recv[block].astype(F32) + minus_recv[block].astype(F32)
        low, high = total[:, :LANES], total[:, LANES:]
        y_keep[block] = jnp.where(y == 0, low, high)
        y_send[block] = jnp.where(y == 0, high, low).astype(BF16)
        crossed[block] = send(y_send.at[block], y_recv.at[block], at_y)

    def emit(block):
        crossed[block].wait_recv()
        out_ref[pl.ds(block * BLOCK, BLOCK), :] = (y_keep[block] + y_recv[block].astype(F32)).astype(BF16)

    early, late = [], []

    def early_begin(block):
        for part, low in ((top, 0), (bottom, half)):
            early_send[part, :] = project(block, cross.at[1 - y], low, low + half).astype(BF16)
            early.append(send(early_send.at[part], early_recv.at[part], at_y))

    def early_middle(block):
        for index, (part, low) in enumerate(((top, 0), (bottom, half))):
            total = project(block, cross.at[y], low, low + half)
            early[index].wait_recv()
            total = total + early_recv[part, :].astype(F32)
            for z_at in range(4):
                early_sum[z_at, part, :] = total[:, z_at * LANES : (z_at + 1) * LANES]
            late_two[part, :] = early_sum[z_two, part, :].astype(BF16)
            if index == 0:
                late.append(send(late_two.at[top], late_two_plus, at_plus))
                late_minus_send[top, :] = early_sum[z_minus, top, :].astype(BF16)
                late.append(send(late_minus_send.at[top], late_minus.at[top], at_minus))
            else:
                late.append(send(late_two.at[bottom], late_two_minus, at_minus))
                late_plus_send[bottom, :] = early_sum[z_plus, bottom, :].astype(BF16)
                late.append(send(late_plus_send.at[bottom], late_plus.at[bottom], at_plus))

    def early_accumulate():
        late[0].wait_recv()
        late_plus_send[top, :] = (early_sum[z_plus, top, :] + late_two_plus[...].astype(F32)).astype(BF16)
        late.append(send(late_plus_send.at[top], late_plus.at[top], at_plus))
        late[2].wait_recv()
        late_minus_send[bottom, :] = (early_sum[z_minus, bottom, :] + late_two_minus[...].astype(F32)).astype(BF16)
        late.append(send(late_minus_send.at[bottom], late_minus.at[bottom], at_minus))

    def early_emit(block):
        for index in (1, 3, 4, 5):
            late[index].wait_recv()
        total = early_sum[z] + late_plus[...].astype(F32) + late_minus[...].astype(F32)
        out_ref[pl.ds(block * BLOCK, BLOCK), :] = total.astype(BF16)

    fetch(6)
    cores = {}
    pl.when(has_left)(lambda: each(to_right, "wait_recv"))
    pieces[0].wait_recv()
    form_rows(0)
    form_rows(1)
    form_rows(2)
    form_rows(3)
    cores[0] = conv(0)
    pieces[1].wait_recv()
    form_rows(4)
    form_rows(5)
    cores[1] = conv(1)
    weight_copy.wait_recv()
    widen(weight_far, 1)
    cores[0].wait_recv()
    begin(0)
    cores[1].wait_recv()
    early_begin(1)
    pieces[2].wait_recv()
    form_rows(6)
    form_rows(7)
    cores[2] = conv(2)
    cores[2].wait_recv()
    begin(2)
    pl.when(has_right)(lambda: each(to_left, "wait_recv"))
    pieces[3].wait_recv()
    form_rows(8)
    form_rows(9)
    cores[3] = conv(3)
    cores[3].wait_recv()
    begin(3)
    accumulate(0)
    accumulate(2)
    accumulate(3)
    early_middle(1)
    finish(0)
    finish(2)
    early_accumulate()
    finish(3)
    emit(0)
    emit(2)
    early_emit(1)
    emit(3)
    pl.when(has_right)(lambda: each(to_right, "wait_send"))
    pl.when(has_left)(lambda: each(to_left, "wait_send"))
    each(pieces + [weight_copy] + list(cores.values()) + early + late, "wait_send")
    for block in (0, 2, 3):
        each(two[block] + plain[block] + added[block] + (crossed[block],), "wait_send")


def body(activations, bases, complement, embedding, filter_taps, projection):
    length, channels = activations.shape
    blocks = length // BLOCK
    copies = 48
    tables = dft_tables(filter_taps.shape[0])
    flip = np.eye(LANES)[::-1].astype(BF16)
    operands = [
        activations, bases.reshape(length // LANES, LANES), complement, embedding, filter_taps, projection,
        jnp.asarray(flip), *[jnp.asarray(t) for t in tables],
    ]
    vmem = pl.BlockSpec(memory_space=pltpu.VMEM)
    return pl.pallas_call(
        kernel,
        out_shape=jax.ShapeDtypeStruct((length, channels), BF16),
        in_specs=[pl.BlockSpec(memory_space=pl.ANY)] * len(operands),
        out_specs=vmem,
        scratch_shapes=[
            (pltpu.SMEM if operand.ndim == 1 else pltpu.VMEM)(operand.shape, operand.dtype) for operand in operands
        ]
        + [
            pltpu.VMEM((2, LANES, LANES), BF16),
            pltpu.VMEM((2, 8, LANES), jnp.int32),
            pltpu.VMEM((length, LANES), BF16),
            pltpu.VMEM((2, LANES, LANES), BF16),
            pltpu.VMEM(projection.shape, BF16),
            pltpu.VMEM((16, 2 * LANES), F32),
            pltpu.VMEM((3, BLOCK, 2 * LANES), F32),
            pltpu.VMEM((length + 2 * LANES, 2 * LANES), BF16),
            pltpu.VMEM((4, 4 * LANES, 2 * LANES), BF16),
            pltpu.VMEM((2, 4 * LANES, 4 * LANES), BF16),
            pltpu.VMEM((blocks, BLOCK, 2 * LANES), BF16),
            pltpu.VMEM((blocks, BLOCK, 2 * LANES), BF16),
            pltpu.VMEM((blocks, BLOCK, 2 * LANES), BF16),
            pltpu.VMEM((blocks, BLOCK // 2, 2 * LANES), BF16),
            pltpu.VMEM((blocks, BLOCK // 2, 2 * LANES), BF16),
            pltpu.VMEM((blocks, BLOCK, 2 * LANES), BF16),
            pltpu.VMEM((blocks, BLOCK, 2 * LANES), BF16),
            pltpu.VMEM((blocks, BLOCK, 2 * LANES), BF16),
            pltpu.VMEM((blocks, BLOCK, 2 * LANES), BF16),
            pltpu.VMEM((blocks, BLOCK, LANES), BF16),
            pltpu.VMEM((blocks, BLOCK, LANES), BF16),
            pltpu.VMEM((blocks, BLOCK, LANES), F32),
            pltpu.VMEM((BLOCK, 4 * LANES), BF16),
            pltpu.VMEM((BLOCK, 4 * LANES), BF16),
            pltpu.VMEM((4, BLOCK, LANES), F32),
            pltpu.VMEM((BLOCK, LANES), BF16),
            pltpu.VMEM((BLOCK // 2, LANES), BF16),
            pltpu.VMEM((BLOCK // 2, LANES), BF16),
            pltpu.VMEM((BLOCK, LANES), BF16),
            pltpu.VMEM((BLOCK, LANES), BF16),
            pltpu.VMEM((BLOCK, LANES), BF16),
            pltpu.VMEM((BLOCK, LANES), BF16),
            pltpu.SemaphoreType.DMA((copies,)),
            pltpu.SemaphoreType.DMA((copies,)),
            pltpu.SemaphoreType.DMA((len(operands),)),
        ],
        compiler_params=pltpu.CompilerParams(
            collective_id=0, has_side_effects=True, vmem_limit_bytes=56 * 1024 * 1024
        ),
    )(*operands)


def solution(mesh):
    placed = (P("seq", "tensor"), P("seq"), P(), P(), P(None, "tensor"), P("tensor", None))
    return jax.shard_map(
        body, mesh=mesh, in_specs=placed, out_specs=P("seq", "tensor"), check_vma=False
    )
```

time: 57.1 us -> 41.7 us (0.73)
  the two profiles are of different devices: /device:TPU:16 before, /device:TPU:0 now
where the time goes in v1:
time: 41.7 us; the launch traced here: 41.6 us
  Pallas kernels  39.9 us (96%)
  local copies, waits for them, and re-layouts  1.67 us (4%)
    pallas_call x1, Pallas kernels, body(): pl.pallas_call(kernel, out_shape=jax.ShapeDtypeStruct((length, channels),...  39.9 us
    unnamed x1, local copies, waits for them, and re-layouts  1.67 us

profile of v1, /device:TPU:0, one launch (start us, length us, event | category | flops | bytes accessed | tf_op | source)
XLA Modules:
  0.0 41.6 jit_solution(8097095676155257981)
XLA Ops:
  0.0 39.9 %shard_map.127 = bf16[1024,128]{1,0:T(8,128)(2,1)} custom-call(bf16[1024,128]{1,0:T(8,128)(2,1)} %acts_hbm.1, s32[8,128]{1,0:T(8,128)} %bitcast.1, s32[5]{0:T(128)} %complement_hbm.1, bf16[5,2048]{1,0:T(8,128)(2,1)} %embedding_hbm.1, bf16[255,128]{1,0:T(8,128)(2,1)} %taps_hbm.1, bf16[128,2048]{1,0:T(8,128)(2,1)} %weight_hbm.1, ...), custom_call_target="tpu_custom_call" | custom-call | tf_op jit(solution)/shard_map/pallas_call | solution.py:368
  39.9 1.7 %copy.15 = bf16[1024,128]{1,0:T(8,128)(2,1)} copy(bf16[1024,128]{1,0:T(8,128)(2,1)} %shard_map.127) | data formatting | bytes 524288

commit v2 on v1

--- a/solution.py
+++ b/solution.py
@@ -64,21 +64,6 @@
     late_plus_send, late_minus_send, late_plus, late_minus,
     send_sem, recv_sem, local_sem,
 ):
-    fetched = []
-    for source, target in (
-        (taps_hbm, taps_ref), (tap_hi_hbm, tap_hi), (tap_lo_hbm, tap_lo), (complement_hbm, complement_ref),
-        (embedding_hbm, embedding_ref), (flip_hbm, flip_ref), (weight_hbm, weight_ref), (bases_hbm, bases_ref),
-        (acts_hbm, acts_ref), (fwd_hi_hbm, fwd_hi), (fwd_lo_hbm, fwd_lo), (inv_hi_hbm, inv_hi), (inv_lo_hbm, inv_lo),
-    ):
-        copy = pltpu.make_async_copy(source, target, local_sem.at[len(fetched)])
-        copy.start()
-        fetched.append(copy)
-
-    def fetch(count):
-        for copy in fetched[:count]:
-            copy.wait()
-        del fetched[:count]
-
     seq, tensor = lax.axis_index("seq"), lax.axis_index("tensor")
     seq_count = lax.axis_size("seq")
     z, y, core = tensor // 4, (tensor // 2) % 2, tensor % 2
@@ -99,6 +84,21 @@
     greet((seq, opposite), at_plus, at_minus, at_core, at_y)
     pl.when(has_right)(lambda: greet((right, tensor), (right, opposite)))
     pl.when(has_left)(lambda: greet((left, tensor), (left, opposite)))
+    fetched = []
+    for source, target in (
+        (taps_hbm, taps_ref), (tap_hi_hbm, tap_hi), (tap_lo_hbm, tap_lo), (complement_hbm, complement_ref),
+        (embedding_hbm, embedding_ref), (flip_hbm, flip_ref), (weight_hbm, weight_ref), (bases_hbm, bases_ref),
+        (acts_hbm, acts_ref), (fwd_hi_hbm, fwd_hi), (fwd_lo_hbm, fwd_lo), (inv_hi_hbm, inv_hi), (inv_lo_hbm, inv_lo),
+    ):
+        copy = pltpu.make_async_copy(source, target, local_sem.at[len(fetched)])
+        copy.start()
+        fetched.append(copy)
+
+    def fetch(count):
+        for copy in fetched[:count]:
+            copy.wait()
+        del fetched[:count]
+
     pl.semaphore_wait(barrier, 5 + 2 * has_right.astype(jnp.int32) + 2 * has_left.astype(jnp.int32))
 
     count = [0]
@@ -321,36 +321,36 @@
     cores[0].wait_recv()
     begin(0)
     cores[1].wait_recv()
-    early_begin(1)
+    begin(1)
     pieces[2].wait_recv()
     form_rows(6)
     form_rows(7)
     cores[2] = conv(2)
     cores[2].wait_recv()
-    begin(2)
+    early_begin(2)
     pl.when(has_right)(lambda: each(to_left, "wait_recv"))
     pieces[3].wait_recv()
     form_rows(8)
     form_rows(9)
     cores[3] = conv(3)
+    accumulate(0)
     cores[3].wait_recv()
     begin(3)
-    accumulate(0)
-    accumulate(2)
+    accumulate(1)
     accumulate(3)
-    early_middle(1)
+    early_middle(2)
     finish(0)
-    finish(2)
+    finish(1)
     early_accumulate()
     finish(3)
     emit(0)
-    emit(2)
-    early_emit(1)
+    emit(1)
+    early_emit(2)
     emit(3)
     pl.when(has_right)(lambda: each(to_right, "wait_send"))
     pl.when(has_left)(lambda: each(to_left, "wait_send"))
     each(pieces + [weight_copy] + list(cores.values()) + early + late, "wait_send")
-    for block in (0, 2, 3):
+    for block in sorted(two):
         each(two[block] + plain[block] + added[block] + (crossed[block],), "wait_send")
 
 
@@ -367,7 +367,7 @@
     vmem = pl.BlockSpec(memory_space=pltpu.VMEM)
     return pl.pallas_call(
         kernel,
-        out_shape=jax.ShapeDtypeStruct((length, channels), BF16),
+        out_shape=pltpu.VMEM((length, channels), BF16),
         in_specs=[pl.BlockSpec(memory_space=pl.ANY)] * len(operands),
         out_specs=vmem,
         scratch_shapes=[

time: 41.7 us -> 38.7 us (0.928)
  Pallas kernels: 39.9 us -> 37.9 us
  local copies, waits for them, and re-layouts: 1.67 us -> 0.71 us
    pallas_call x1, Pallas kernels: 39.9 us -> 37.9 us  [body(): pl.pallas_call(kernel, out_shape=pltpu.VMEM((length, channels), BF16), in...]
    unnamed x1, local copies, waits for them, and re-layouts: 1.67 us -> 0.71 us
where the time goes in v2:
time: 38.7 us; the launch traced here: 38.6 us
  Pallas kernels  37.9 us (98%)
  local copies, waits for them, and re-layouts  0.71 us (2%)
    pallas_call x1, Pallas kernels, body(): pl.pallas_call(kernel, out_shape=pltpu.VMEM((length, channels), BF16), in...  37.9 us

profile of v2, /device:TPU:0, one launch (start us, length us, event | category | flops | bytes accessed | tf_op | source)
XLA Modules:
  0.0 38.6 jit_solution(1864901210360777289)
XLA Ops:
  0.0 37.9 %shard_map.127 = bf16[1024,128]{1,0:T(8,128)(2,1)S(1)} custom-call(bf16[1024,128]{1,0:T(8,128)(2,1)} %acts_hbm.1, s32[8,128]{1,0:T(8,128)} %bitcast.1, s32[5]{0:T(128)} %complement_hbm.1, bf16[5,2048]{1,0:T(8,128)(2,1)} %embedding_hbm.1, bf16[255,128]{1,0:T(8,128)(2,1)} %taps_hbm.1, bf16[128,2048]{1,0:T(8,128)(2,1)} %weight_hbm.1, ...), custom_call_target="tpu_custom_call" | custom-call | tf_op jit(solution)/shard_map/pallas_call | solution.py:368
  37.9 0.7 %copy.15 = bf16[1024,128]{1,0:T(8,128)(2,1)} copy(bf16[1024,128]{1,0:T(8,128)(2,1)S(1)} %shard_map.127) | data formatting | bytes 524288

commit v3 on v2

--- a/solution.py
+++ b/solution.py
@@ -60,7 +60,7 @@
     halo, bases_halo, mirror, mirror_halo, weight_far,
     table, coef, rows, wide, cross, near, far,
     two_send, two_plus, two_minus, plus_send, minus_send, plus_recv, minus_recv, y_send, y_recv, y_keep,
-    early_send, early_recv, early_sum, late_two, late_two_plus, late_two_minus,
+    early_send, early_recv, early_sum, late_two, late_far,
     late_plus_send, late_minus_send, late_plus, late_minus,
     send_sem, recv_sem, local_sem,
 ):
@@ -73,6 +73,7 @@
     z_plus, z_minus, z_two = lax.rem(z + 1, 4), lax.rem(z + 3, 4), lax.rem(z + 2, 4)
     at_plus = (seq, z_plus * 4 + y * 2 + core)
     at_minus = (seq, z_minus * 4 + y * 2 + core)
+    at_two = (seq, z_two * 4 + y * 2 + core)
     at_core = (seq, z * 4 + y * 2 + (1 - core))
     at_y = (seq, z * 4 + (1 - y) * 2 + core)
     barrier = pltpu.get_barrier_semaphore()
@@ -81,7 +82,7 @@
         for partner in partners:
             pl.semaphore_signal(barrier, inc=1, device_id=partner, device_id_type=MESH)
 
-    greet((seq, opposite), at_plus, at_minus, at_core, at_y)
+    greet((seq, opposite), at_plus, at_minus, at_core, at_y, at_two)
     pl.when(has_right)(lambda: greet((right, tensor), (right, opposite)))
     pl.when(has_left)(lambda: greet((left, tensor), (left, opposite)))
     fetched = []
@@ -99,7 +100,7 @@
             copy.wait()
         del fetched[:count]
 
-    pl.semaphore_wait(barrier, 5 + 2 * has_right.astype(jnp.int32) + 2 * has_left.astype(jnp.int32))
+    pl.semaphore_wait(barrier, 6 + 2 * has_right.astype(jnp.int32) + 2 * has_left.astype(jnp.int32))
 
     count = [0]
 
@@ -280,27 +281,15 @@
             for z_at in range(4):
                 early_sum[z_at, part, :] = total[:, z_at * LANES : (z_at + 1) * LANES]
             late_two[part, :] = early_sum[z_two, part, :].astype(BF16)
-            if index == 0:
-                late.append(send(late_two.at[top], late_two_plus, at_plus))
-                late_minus_send[top, :] = early_sum[z_minus, top, :].astype(BF16)
-                late.append(send(late_minus_send.at[top], late_minus.at[top], at_minus))
-            else:
-                late.append(send(late_two.at[bottom], late_two_minus, at_minus))
-                late_plus_send[bottom, :] = early_sum[z_plus, bottom, :].astype(BF16)
-                late.append(send(late_plus_send.at[bottom], late_plus.at[bottom], at_plus))
-
-    def early_accumulate():
-        late[0].wait_recv()
-        late_plus_send[top, :] = (early_sum[z_plus, top, :] + late_two_plus[...].astype(F32)).astype(BF16)
-        late.append(send(late_plus_send.at[top], late_plus.at[top], at_plus))
-        late[2].wait_recv()
-        late_minus_send[bottom, :] = (early_sum[z_minus, bottom, :] + late_two_minus[...].astype(F32)).astype(BF16)
-        late.append(send(late_minus_send.at[bottom], late_minus.at[bottom], at_minus))
+            late.append(send(late_two.at[part], late_far.at[part], at_two))
+            late_plus_send[part, :] = early_sum[z_plus, part, :].astype(BF16)
+            late.append(send(late_plus_send.at[part], late_plus.at[part], at_plus))
+            late_minus_send[part, :] = early_sum[z_minus, part, :].astype(BF16)
+            late.append(send(late_minus_send.at[part], late_minus.at[part], at_minus))
 
     def early_emit(block):
-        for index in (1, 3, 4, 5):
-            late[index].wait_recv()
-        total = early_sum[z] + late_plus[...].astype(F32) + late_minus[...].astype(F32)
+        each(late, "wait_recv")
+        total = early_sum[z] + late_plus[...].astype(F32) + late_minus[...].astype(F32) + late_far[...].astype(F32)
         out_ref[pl.ds(block * BLOCK, BLOCK), :] = total.astype(BF16)
 
     fetch(6)
@@ -338,10 +327,9 @@
     begin(3)
     accumulate(1)
     accumulate(3)
+    finish(0)
     early_middle(2)
-    finish(0)
     finish(1)
-    early_accumulate()
     finish(3)
     emit(0)
     emit(1)
@@ -400,8 +388,7 @@
             pltpu.VMEM((BLOCK, 4 * LANES), BF16),
             pltpu.VMEM((4, BLOCK, LANES), F32),
             pltpu.VMEM((BLOCK, LANES), BF16),
-            pltpu.VMEM((BLOCK // 2, LANES), BF16),
-            pltpu.VMEM((BLOCK // 2, LANES), BF16),
+            pltpu.VMEM((BLOCK, LANES), BF16),
             pltpu.VMEM((BLOCK, LANES), BF16),
             pltpu.VMEM((BLOCK, LANES), BF16),
             pltpu.VMEM((BLOCK, LANES), BF16),

time: 38.7 us -> 39.2 us (1.013)
  Pallas kernels: 37.9 us -> 38.4 us
    pallas_call x1, Pallas kernels: 37.9 us -> 38.4 us  [body(): pl.pallas_call(kernel, out_shape=pltpu.VMEM((length, channels), BF16), in...]
where the time goes in v3:
time: 39.2 us; the launch traced here: 39.1 us
  Pallas kernels  38.4 us (98%)
  local copies, waits for them, and re-layouts  0.71 us (2%)
    pallas_call x1, Pallas kernels, body(): pl.pallas_call(kernel, out_shape=pltpu.VMEM((length, channels), BF16), in...  38.4 us

profile of v3, /device:TPU:0, one launch (start us, length us, event | category | flops | bytes accessed | tf_op | source)
XLA Modules:
  0.0 39.1 jit_solution(11989552487744692789)
XLA Ops:
  0.0 38.4 %shard_map.127 = bf16[1024,128]{1,0:T(8,128)(2,1)S(1)} custom-call(bf16[1024,128]{1,0:T(8,128)(2,1)} %acts_hbm.1, s32[8,128]{1,0:T(8,128)} %bitcast.1, s32[5]{0:T(128)} %complement_hbm.1, bf16[5,2048]{1,0:T(8,128)(2,1)} %embedding_hbm.1, bf16[255,128]{1,0:T(8,128)(2,1)} %taps_hbm.1, bf16[128,2048]{1,0:T(8,128)(2,1)} %weight_hbm.1, ...), custom_call_target="tpu_custom_call" | custom-call | tf_op jit(solution)/shard_map/pallas_call | solution.py:356
  38.4 0.7 %copy.15 = bf16[1024,128]{1,0:T(8,128)(2,1)} copy(bf16[1024,128]{1,0:T(8,128)(2,1)S(1)} %shard_map.127) | data formatting | bytes 524288

commit v4 on v2

--- a/solution.py
+++ b/solution.py
@@ -229,11 +229,10 @@
     two, plain, added, crossed = {}, {}, {}, {}
 
     def begin(block):
-        two_send[block] = project(block, wide.at[z_two], 0, BLOCK).astype(BF16)
-        two[block] = (
-            send(two_send.at[block, top], two_plus.at[block], at_plus),
-            send(two_send.at[block, bottom], two_minus.at[block], at_minus),
-        )
+        two_send[block, :half, :] = project(block, wide.at[z_two], 0, half).astype(BF16)
+        upper = send(two_send.at[block, top], two_plus.at[block], at_plus)
+        two_send[block, half:, :] = project(block, wide.at[z_two], half, BLOCK).astype(BF16)
+        two[block] = (upper, send(two_send.at[block, bottom], two_minus.at[block], at_minus))
         plus_send[block, half:, :] = project(block, wide.at[z_plus], half, BLOCK).astype(BF16)
         plain_plus = send(plus_send.at[block, bottom], plus_recv.at[block, bottom], at_plus)
         minus_send[block, :half, :] = project(block, wide.at[z_minus], 0, half).astype(BF16)

time: 38.7 us -> 39.1 us (1.010)
  Pallas kernels: 37.9 us -> 38.3 us
where the time goes in v4:
time: 39.1 us; the launch traced here: 39 us
  Pallas kernels  38.3 us (98%)
  local copies, waits for them, and re-layouts  0.71 us (2%)
    pallas_call x1, Pallas kernels, body(): pl.pallas_call(kernel, out_shape=pltpu.VMEM((length, channels), BF16), in...  38.3 us

profile of v4, /device:TPU:0, one launch (start us, length us, event | category | flops | bytes accessed | tf_op | source)
XLA Modules:
  0.0 39.0 jit_solution(16060545870259390321)
XLA Ops:
  0.0 38.3 %shard_map.127 = bf16[1024,128]{1,0:T(8,128)(2,1)S(1)} custom-call(bf16[1024,128]{1,0:T(8,128)(2,1)} %acts_hbm.1, s32[8,128]{1,0:T(8,128)} %bitcast.1, s32[5]{0:T(128)} %complement_hbm.1, bf16[5,2048]{1,0:T(8,128)(2,1)} %embedding_hbm.1, bf16[255,128]{1,0:T(8,128)(2,1)} %taps_hbm.1, bf16[128,2048]{1,0:T(8,128)(2,1)} %weight_hbm.1, ...), custom_call_target="tpu_custom_call" | custom-call | tf_op jit(solution)/shard_map/pallas_call | solution.py:367
  38.3 0.7 %copy.15 = bf16[1024,128]{1,0:T(8,128)(2,1)} copy(bf16[1024,128]{1,0:T(8,128)(2,1)S(1)} %shard_map.127) | data formatting | bytes 524288
